TPU v7x, 128 devices: a whole 4x4x4 slice. The times are simulated.
128 devices in a mesh: space: 16 (over y, x_lo, core), chan: 4 (over z), filt: 2 (over x_hi).
Axes of the slice: x: 4 (x_hi: 2, x_lo: 2; x = x_hi * 2 + x_lo), y: 4, z: 4, core: 2. Of those that a mesh axis runs over, the one named last changes fastest.
Arguments:
- volume: bfloat16 [64, 32, 32, 512], P('space', None, None, 'chan'), may hold values from -6 to 6
- kernel_one: bfloat16 [27, 512, 1024], P(None, 'chan', 'filt'), may hold values from -0.0546875 to 0.0546875
- kernel_two: bfloat16 [27, 1024, 1024], P(None, 'filt', 'chan'), may hold values from -0.0390625 to 0.0390625
- upstream: bfloat16 [16, 8, 8, 1024], P('space', None, None, ('chan', 'filt')), may hold values from -0.23925781 to 0.23925781
Outputs:
- features: float32 [16, 8, 8, 1024], P('space', None, None, ('chan', 'filt'))
- kernel_one_grad: float32 [27, 512, 1024], P(None, ('chan', 'space'), 'filt')
- kernel_two_grad: float32 [27, 1024, 1024], P(None, ('filt', 'space'), 'chan')
All inputs are finite; a program needn't handle non-finite values.
Results may differ from a plain program's by a relative error of at most 0.005.
Values may be sent and summed in bfloat16 or wider, within the bound.
A program may use at most 128 MiB of HBM per device.

v0:
```python
import jax
import jax.numpy as jnp
from jax import lax
from jax.sharding import PartitionSpec as P

LEAKY_SLOPE = 0.3


def passed_along(block, axis, distance):
    devices = range(lax.axis_size(axis))
    route = [(i - distance, i) for i in devices if i - distance in devices]
    return lax.ppermute(block, axis, route)


def patches(padded, depth_out, side_out):
    channels = padded.shape[3]
    depth_pad = 2 * depth_out + 2 - padded.shape[0]
    row_pad = 2 * side_out + 2 - padded.shape[1]
    col_pad = 2 * side_out + 2 - padded.shape[2]
    even = jnp.pad(padded, ((0, depth_pad), (0, row_pad), (0, col_pad), (0, 0)))
    phases = even.reshape(depth_out + 1, 2, side_out + 1, 2, side_out + 1, 2, channels)
    pieces = []
    for depth_tap in range(3):
        for row_tap in range(3):
            for col_tap in range(3):
                pieces.append(
                    phases[
                        depth_tap // 2 : depth_tap // 2 + depth_out,
                        depth_tap % 2,
                        row_tap // 2 : row_tap // 2 + side_out,
                        row_tap % 2,
                        col_tap // 2 : col_tap // 2 + side_out,
                        col_tap % 2,
                        :,
                    ]
                )
    return jnp.stack(pieces, axis=3).reshape(depth_out * side_out * side_out, 27 * channels)


def spread(columns, depth_out, side_out):
    channels = columns.shape[1] // 27
    blocks = columns.reshape(depth_out, side_out, side_out, 27, channels)
    grids = {}
    tap_index = 0
    for depth_tap in range(3):
        for row_tap in range(3):
            for col_tap in range(3):
                placed = jnp.pad(
                    blocks[:, :, :, tap_index, :],
                    (
                        (depth_tap // 2, 1 - depth_tap // 2),
                        (row_tap // 2, 1 - row_tap // 2),
                        (col_tap // 2, 1 - col_tap // 2),
                        (0, 0),
                    ),
                )
                label = (depth_tap % 2, row_tap % 2, col_tap % 2)
                grids[label] = placed if label not in grids else grids[label] + placed
                tap_index += 1
    stacked = jnp.stack(
        [
            jnp.stack(
                [
                    jnp.stack([grids[depth_par, row_par, col_par] for col_par in range(2)], 0)
                    for row_par in range(2)
                ],
                0,
            )
            for depth_par in range(2)
        ],
        0,
    )
    woven = jnp.transpose(stacked, (3, 0, 4, 1, 5, 2, 6)).reshape(
        2 * depth_out + 2, 2 * side_out + 2, 2 * side_out + 2, channels
    )
    return woven[: 2 * depth_out + 1, : 2 * side_out + 1, : 2 * side_out + 1]


def local(volume, kernel_one, kernel_two, upstream):
    planes = volume.shape[0]
    side_len = volume.shape[1]
    cin_local = volume.shape[3]
    mid_local = kernel_one.shape[2]
    out_local = kernel_two.shape[2]
    planes_mid = planes // 2
    side_mid = side_len // 2
    planes_out = planes_mid // 2
    side_out = side_mid // 2
    volume_below = passed_along(volume[planes - 1 :], "space", 1)
    padded = jnp.pad(jnp.concatenate([volume_below, volume], 0), ((0, 0), (1, 0), (1, 0), (0, 0)))
    patch_one = patches(padded, planes_mid, side_mid)
    partial_value = jnp.dot(
        patch_one, kernel_one.reshape(27 * cin_local, mid_local), preferred_element_type=jnp.float32
    )
    mixed_sum = lax.psum(partial_value, "chan")
    hidden = jnp.where(mixed_sum > 0, mixed_sum, LEAKY_SLOPE * mixed_sum).astype(jnp.bfloat16)
    hidden_vol = hidden.reshape(planes_mid, side_mid, side_mid, mid_local)
    hidden_below = passed_along(hidden_vol[planes_mid - 1 :], "space", 1)
    hidden_padded = jnp.pad(
        jnp.concatenate([hidden_below, hidden_vol], 0), ((0, 0), (1, 0), (1, 0), (0, 0))
    )
    patch_two = patches(hidden_padded, planes_out, side_out)
    kernel_flat = kernel_two.reshape(27 * mid_local, out_local)
    partial_out = jnp.dot(patch_two, kernel_flat, preferred_element_type=jnp.float32).reshape(
        planes_out, side_out, side_out, out_local
    )
    features = lax.psum_scatter(partial_out, "filt", scatter_dimension=3, tiled=True)
    seed_block = lax.all_gather(upstream, "filt", axis=3, tiled=True)
    term_two = lax.dot_general(
        patch_two,
        seed_block.reshape(-1, out_local),
        (((0,), (0,)), ((), ())),
        preferred_element_type=jnp.float32,
    ).reshape(27, mid_local, out_local)
    kernel_two_grad = lax.psum_scatter(term_two, "space", scatter_dimension=1, tiled=True)
    seed_after = passed_along(seed_block, "space", -1)
    extended = jnp.concatenate([seed_block, seed_after], 0)
    back_columns = lax.dot_general(
        extended.reshape(-1, out_local),
        kernel_flat,
        (((1,), (1,)), ((), ())),
        preferred_element_type=jnp.float32,
    )
    back_part = spread(back_columns, planes_out + 1, side_out)[1 : planes_mid + 1, 1:, 1:]
    back_flat = back_part.reshape(-1, mid_local)
    back_sum = lax.psum(back_flat, "chan")
    delta_full = (back_sum * jnp.where(mixed_sum > 0, 1.0, LEAKY_SLOPE)).astype(jnp.bfloat16)
    term_one = lax.dot_general(
        patch_one, delta_full, (((0,), (0,)), ((), ())), preferred_element_type=jnp.float32
    ).reshape(27, cin_local, mid_local)
    kernel_one_grad = lax.psum_scatter(term_one, "space", scatter_dimension=1, tiled=True)
    return (features, kernel_one_grad, kernel_two_grad)


def solution(mesh):
    return jax.shard_map(
        local,
        mesh=mesh,
        in_specs=(
            P("space", None, None, "chan"),
            P(None, "chan", "filt"),
            P(None, "filt", "chan"),
            P("space", None, None, ("chan", "filt")),
        ),
        out_specs=(
            P("space", None, None, ("chan", "filt")),
            P(None, ("chan", "space"), "filt"),
            P(None, ("filt", "space"), "chan"),
        ),
        check_vma=False,
    )
```

profile of v0, /device:TPU:0, one launch (start us, length us, event | category | flops | bytes accessed | tf_op | source)
XLA Modules:
  0.0 451.8 jit_solution(5119002096637190965)
XLA Ops:
  7.2 0.0 copy-start
  7.2 0.0 all-reduce.34.cloned.1.call-start
  7.2 6.3 %all_gather.3 = bf16[1,8,8,256]{3,2,1,0:T(8,128)(2,1)S(1)} all-gather(bf16[1,8,8,128]{3,2,1,0:T(8,128)(2,1)} %param.7), channel_id=1, replica_groups=mesh['space'=16,'chan'=4,'filt'=2] {'filt'}, dimensions={3}, use_global_device_ids=true | all-gather | bytes 49152 | tf_op jit(solution)/shard_map/all_gather | solution.py:108
  13.5 1.3 collective-permute-start.2
  14.8 1.7 slice.257
  16.5 3.7 collective-permute-start
  20.2 0.0 collective-permute-done.2
  20.2 5.4 %fusion = f32[2,8,8,27,512]{4,2,3,1,0:T(8,128)S(1)} fusion(bf16[27,512,256]{2,1,0:T(8,128)(2,1)} %param.6, bf16[1,8,8,256]{3,2,1,0:T(8,128)(2,1)S(1)} %collective-permute-done.2, bf16[1,8,8,256]{3,2,1,0:T(8,128)(2,1)S(1)} %all_gather.3), kind=kOutput, calls=%fused_computation.1 | convolution fusion | flops 906100736 | bytes 14221312 | tf_op jit(solution)/shard_map/dot_general | solution.py:118
  25.6 0.5 slice_bitcast_fusion.26
  26.2 0.2 slice_bitcast_fusion.25
  26.4 0.5 add_bitcast_fusion.5
  26.9 0.3 maximum_bitcast_fusion.3
  27.2 0.3 add_bitcast_fusion.3
  27.4 0.2 maximum_bitcast_fusion.4
  27.6 0.8 maximum_bitcast_fusion.1
  28.4 0.3 add_bitcast_fusion.1
  28.7 0.2 maximum_bitcast_fusion.5
  28.9 0.2 pad_bitcast_fusion
  29.1 0.2 maximum_bitcast_fusion.6
  29.3 0.8 maximum_bitcast_fusion.2
  30.1 0.9 maximum_bitcast_fusion
  31.0 5.8 %copy.1711 = f32[3,2,9,2,9,2,512]{6,5,4,3,2,1,0:T(2,128)} copy(f32[3,2,9,2,9,2,512]{6,4,2,0,5,3,1:T(8,128)S(1)} %maximum_bitcast_fusion) | data formatting | bytes 7962624 | tf_op jit(solution)/shard_map/transpose | solution.py:73
  36.8 18.2 %reshape.62 = f32[6,18,18,512]{3,2,1,0:T(8,128)} reshape(f32[3,2,9,2,9,2,512]{6,5,4,3,2,1,0:T(2,128)} %copy.1711) | data formatting | bytes 7962624 | tf_op jit(solution)/shard_map/reshape | solution.py:73
  55.0 2.7 slice.424
  57.7 0.0 collective-permute-done
  57.7 1.9 fusion.16
  59.5 1.7 pad.106
  61.2 4.8 %reshape.55 = bf16[3,2,17,2,17,2,128]{6,5,4,3,2,1,0:T(2,128)(2,1)} reshape(bf16[6,34,34,128]{3,2,1,0:T(8,128)(2,1)} %pad.106) | data formatting | bytes 3551232 | tf_op jit(solution)/shard_map/reshape | solution.py:21
  66.1 3.4 fusion.37
  69.5 5.5 %fusion.36 = (bf16[2,1,16,1,16,1,128]{6,5,4,3,2,1,0:T(2,128)(2,1)S(1)}, bf16[2,1,16,1,16,1,128]{6,5,4,3,2,1,0:T(2,128)(2,1)S(1)}, bf16[2,1,16,1,16,1,128]{6,5,4,...) fusion(bf16[3,2,17,2,17,2,128]{6,5,4,3,2,1,0:T(2,128)(2,1)S(1)}, ...), kind=kLoop, calls=%fused_computation.141 | loop fusion | bytes 4980736 | tf_op jit(solution)/shard_map/slice | solution.py:27
  76.0 4.0 copy.1680
  80.0 0.0 copy-start.3
  80.0 0.0 copy-done
  80.0 3.1 fusion.2
  83.2 0.0 all-reduce.34.cloned.1.call-update
  83.2 0.0 reduce-scatter.4.cloned.1.call-start
  83.3 61.6 %all-reduce.34.cloned.1.call-done = (f32[512,512]{1,0:T(8,128)}, f32[512,512]{1,0:T(8,128)}) async-done(((f32[512,512]{1,0:T(8,128)}, f32[512,512]{1,0:T(8,128)}), (f32[512,512]{1,0:T(8,128)}, f32[512,512]{1,0:T(8,128)})) %all-reduce.34.cloned.1.call-update) | async-done | bytes 2097168 | tf_op jit(solution)/shard_map/psum | solution.py:95
  144.9 1.4 fusion.22
  146.2 0.0 copy-start.5
  146.3 0.8 copy-done.5
  147.1 1.3 copy.1681
  148.3 2.5 collective-permute-start.1
  150.9 7.4 %copy.1863 = bf16[64,8,27,128]{3,1,2,0:T(8,128)(2,1)} copy(bf16[64,8,27,128]{3,2,1,0:T(8,128)(2,1)} %bitcast.300) | data formatting | bytes 7077888
  158.3 5.7 %copy.1684 = bf16[3456,512]{1,0:T(8,128)(2,1)} copy(bf16[3456,512]{0,1:T(8,128)(2,1)} %bitcast.304) | data formatting | bytes 7077888 | tf_op jit(solution)/shard_map/dot_general | solution.py:128
  164.1 1.6 copy.1682
  165.6 0.0 collective-permute-done.1
  165.7 2.1 fusion.18
  167.8 1.6 pad.108
  169.3 4.0 reshape.59
  173.4 2.7 fusion.39
  176.1 3.1 fusion.38
  179.8 0.1 copy.1864
  179.9 1.3 copy-done.4
  181.2 4.9 %convolution_bitcast_fusion = f32[1,8,8,256]{3,2,1,0:T(8,128)} fusion(bf16[8,8,13824]{2,1,0:T(8,128)(2,1)S(1)} %bitcast.301, bf16[13824,256,1]{1,0,2:T(8,128)(2,1)} %bitcast.305), kind=kOutput, calls=%fused_computation.34 | convolution fusion | flops 452984832 | bytes 8912896 | tf_op jit(solution)/shard_map/dot_general | solution.py:104
  186.1 0.0 reduce-scatter.4.cloned.1.call-update
  186.1 0.0 reduce-scatter.6.cloned.1.call-start
  186.2 7.5 %fusion.24 = f32[27,128,512]{2,1,0:T(8,128)} fusion(bf16[27,128,512]{2,1,0:T(8,128)(2,1)} %bitcast.303, f32[512,512]{1,0:T(8,128)} %get-tuple-element.4, f32[512,512]{1,0:T(8,128)} %get-tuple-element.3), kind=kOutput, calls=%fused_computation.47 | convolution fusion | flops 1812987904 | bytes 12713984 | tf_op jit(solution)/shard_map/dot_general | solution.py:128
  193.6 0.0 reduce-scatter.6.cloned.1.call-update
  193.7 0.0 reduce-scatter.8.cloned.1.call-start
  193.7 8.6 %fusion.13 = f32[27,512,256]{2,1,0:T(8,128)} fusion(bf16[8,27,8,512]{3,2,1,0:T(8,128)(2,1)} %bitcast.302, bf16[1,8,8,256]{3,2,1,0:T(8,128)(2,1)} %copy-done.7), kind=kOutput, calls=%fused_computation.21 | convolution fusion | flops 452984832 | bytes 15958016 | tf_op jit(solution)/shard_map/dot_general | solution.py:109
  202.3 0.0 reduce-scatter.8.cloned.1.call-update
  202.3 0.0 reduce-scatter.4.cloned.1.call-done
  202.4 85.0 %reduce-scatter.6.cloned.1.call-done = f32[27,8,512]{2,1,0:T(8,128)} async-done(((f32[27,128,512]{2,1,0:T(8,128)}), f32[27,8,512]{2,1,0:T(8,128)}) %reduce-scatter.6.cloned.1.call-update) | async-done | bytes 442384 | tf_op jit(solution)/shard_map/reduce_scatter | solution.py:131
  287.3 157.6 %reduce-scatter.8.cloned.1.call-done = f32[27,32,256]{2,1,0:T(8,128)} async-done(((f32[27,512,256]{2,1,0:T(8,128)}), f32[27,32,256]{2,1,0:T(8,128)}) %reduce-scatter.8.cloned.1.call-update) | async-done | bytes 884752 | tf_op jit(solution)/shard_map/reduce_scatter | solution.py:115
  (65 shorter events, 1.2 us)
Async XLA Ops:
  7.2 72.9 %copy-start = (bf16[27,128,512]{2,1,0:T(8,128)(2,1)S(1)}, bf16[27,128,512]{2,1,0:T(8,128)(2,1)}, u32[]{:S(2)}) copy-start(bf16[27,128,512]{2,1,0:T(8,128)(2,1)} %param.5) | copy-start | bytes 10616836
  7.2 137.7 %all-reduce.34.cloned.1.call-start = ((), (), s32[]{:S(2)}) async-start(), calls=%async_computation.6 | async-start | bytes 4194304 | tf_op jit(solution)/shard_map/psum | solution.py:95
  13.5 12.1 %copy-start.7 = (bf16[1,8,8,256]{3,2,1,0:T(8,128)(2,1)}, bf16[1,8,8,256]{3,2,1,0:T(8,128)(2,1)S(1)}, u32[]{:S(2)}) copy-start(bf16[1,8,8,256]{3,2,1,0:T(8,128)(2,1)S(1)} %all_gather.3) | copy-start | bytes 98308
  13.5 6.7 %collective-permute-start.2 = (bf16[1,8,8,256]{3,2,1,0:T(8,128)(2,1)S(1)}, bf16[1,8,8,256]{3,2,1,0:T(8,128)(2,1)S(1)}, u32[]{:S(2)}, u32[]{:S(2)}) collective-permute-start(bf16[1,8,8,256]{3,2,1,0:T(8,128)(2,1)S(1)} %all_gather.3), channel_id=1, source_target_pairs={{8,0},{16,8},{24,16},{32,24},{40,32},{48,40},{56,48},{64,56},{72,6... | collective-permute-start | bytes 98312 | tf_op jit(solution)/shard_map/ppermute | solution.py:12
  16.5 41.2 %collective-permute-start = (bf16[1,32,32,128]{3,2,1,0:T(8,128)(2,1)}, bf16[1,32,32,128]{3,2,1,0:T(8,128)(2,1)}, u32[]{:S(2)}, u32[]{:S(2)}) collective-permute-start(bf16[1,32,32,128]{3,2,1,0:T(8,128)(2,1)} %slice.257), channel_id=1, source_target_pairs={{0,8},{8,16},{16,24},{24,32},{32,40},{40,48},{48,56},{56,64},{64,7... | collective-permute-start | bytes 786440 | tf_op jit(solution)/shard_map/ppermute | solution.py:12
  55.0 2.7 copy-start.6
  66.1 3.4 copy-start.1
  80.0 3.2 copy-start.3
  83.2 119.1 %reduce-scatter.4.cloned.1.call-start = ((), (), s32[]{:S(2)}) async-start(), calls=%async_computation.3 | async-start | bytes 98304 | tf_op jit(solution)/shard_map/reduce_scatter | solution.py:107
  146.2 0.8 copy-start.5
  148.3 17.3 %collective-permute-start.1 = (bf16[1,16,16,512]{3,0,2,1:T(2,128)(2,1)}, bf16[1,16,16,512]{3,0,2,1:T(2,128)(2,1)}, u32[]{:S(2)}, u32[]{:S(2)}) collective-permute-start(bf16[1,16,16,512]{3,0,2,1:T(2,128)(2,1)} %copy.1681), channel_id=1, source_target_pairs={{0,8},{8,16},{16,24},{24,32},{32,40},{40,48},{48,56},{56,64},{64,7... | collective-permute-start | bytes 786440 | tf_op jit(solution)/shard_map/ppermute | solution.py:12
  173.4 2.7 copy-start.2
  179.9 1.3 copy-start.4
  186.1 101.2 %reduce-scatter.6.cloned.1.call-start = ((), (), s32[]{:S(2)}) async-start(), calls=%async_computation.4 | async-start | bytes 7520256 | tf_op jit(solution)/shard_map/reduce_scatter | solution.py:131
  193.7 251.2 %reduce-scatter.8.cloned.1.call-start = ((), (), s32[]{:S(2)}) async-start(), calls=%async_computation.5 | async-start | bytes 15040512 | tf_op jit(solution)/shard_map/reduce_scatter | solution.py:115
Sparse Core Ops, SparseCore 0:
  83.3 61.5 all-reduce.33
  186.2 13.8 reduce-scatter.3
  203.3 83.9 reduce-scatter.5
  290.2 154.6 reduce-scatter.7
where the time goes:
time: 460 us; the launch traced here: 452 us
  waiting for transfers between devices  304 us (66%)
  local copies, waits for them, and re-layouts  79.4 us (17%)
  matrix products  29.5 us (6%)
  between operations  14.8 us (3%)
  other arithmetic  9.8 us (2%)
  starting transfers between devices  7.7 us (2%)
  blocking collectives  6.28 us (1%)
    reduce_scatter x1, waiting for transfers between devices, local(): lax.psum_scatter(term_two, 'space', scatter_dimension=1, tiled=True)  158 us
    reduce_scatter x1, waiting for transfers between devices, local(): lax.psum_scatter(term_one, 'space', scatter_dimension=1, tiled=True)  85 us
    psum x1, waiting for transfers between devices, local(): mixed_sum = lax.psum(partial_value, 'chan')  61.6 us
    reshape x1, local copies, waits for them, and re-layouts, spread(): jnp.transpose(stacked, (3, 0, 4, 1, 5, 2, 6))  18.2 us
    slice x4, local copies, waits for them, and re-layouts, patches(): phases[depth_tap // 2:depth_tap // 2 + depth_out, depth_tap % 2, row_tap...  14.8 us
    unnamed x69, local copies, waits for them, and re-layouts  10.6 us
  transfers between devices with their start and end apart: 7, of which 3 were waited for; matrix products, arithmetic and copies ran while one was open for 15% of the time, Pallas kernels for 0%

commit v1 on v0

v1 whole, which is shorter than its diff:
```python
import jax
import jax.numpy as jnp
from jax import lax
from jax.experimental import pallas as pl
from jax.experimental.pallas import tpu as pltpu
from jax.sharding import PartitionSpec as P

SLOPE = 0.3
F32, BF16 = jnp.float32, jnp.bfloat16
MESH = pl.DeviceIdType.MESH
NMSG = 64


def tap_parts(tap):
    return tap // 9, (tap // 3) % 3, tap % 3


def tap_phase(tap):
    a, b, c = tap_parts(tap)
    return ((a != 1) * 2 + (b != 1)) * 2 + (c != 1)


def tap_shift(tap):
    return tuple(int(v == 0) for v in tap_parts(tap))


def body(
    vol, k1, k2, up, feat_o, g1_o, g2_o,
    vol_v, halo_v, k1_v, k2_v, pf, patch, patch_t,
    up_all, up_f, up_s,
    part, mr1, mr2, bpart, bs1, bs2, br1, br2,
    hid, dlt,
    acc, ksend, krecv, accx, xs4, xr4, xs1, xr1, ys1, yr1, ys2, yr2,
    gh, hh, hp, fs, fp, fr, fx, fxr,
    lsem, ssem, rsem,
):
    s, z, h = lax.axis_index("space"), lax.axis_index("chan"), lax.axis_index("filt")
    k, pair = lax.rem(s, 2), lax.div(s, 2)
    xl, y = lax.rem(pair, 2), lax.div(pair, 2)
    zp, zm, z2 = lax.rem(z + 1, 4), lax.rem(z + 3, 4), lax.rem(z + 2, 4)
    yp, ym, y2 = lax.rem(y + 1, 4), lax.rem(y + 3, 4), lax.rem(y + 2, 4)
    sib = {"space": s + 1 - 2 * k}
    xpt = {"space": y * 4 + (1 - xl) * 2 + k}
    hpt = {"filt": 1 - h}
    yup, ydn, yfar = ({"space": v * 4 + xl * 2 + k} for v in (yp, ym, y2))
    zup, zdn = {"chan": zp}, {"chan": zm}
    nxt, prv = {"space": lax.rem(s + 1, 16)}, {"space": lax.rem(s + 15, 16)}

    msgs = {}

    def send(name, src, dst, device):
        i = len(msgs)
        msgs[name] = pltpu.make_async_remote_copy(
            src_ref=src, dst_ref=dst, send_sem=ssem.at[i], recv_sem=rsem.at[i], device_id=device, device_id_type=MESH
        )
        msgs[name].start()

    def got(name):
        msgs[name].wait_recv()

    def lanes(q):
        return pl.ds(pl.multiple_of(q * 128, 128), 128)

    loads = [
        pltpu.make_async_copy(vol, vol_v, lsem.at[0]),
        pltpu.make_async_copy(up, up_all.at[h, s], lsem.at[1]),
        pltpu.make_async_copy(k1, k1_v, lsem.at[2]),
        pltpu.make_async_copy(k2, k2_v, lsem.at[3]),
    ]
    for copy in loads:
        copy.start()

    barrier = pltpu.get_barrier_semaphore()
    around = (sib, xpt, hpt, yup, ydn, yfar, zup, zdn, nxt, prv)
    for device in around:
        pl.semaphore_signal(barrier, inc=1, device_id=device, device_id_type=MESH)
    pl.semaphore_wait(barrier, len(around))

    send("halo", vol.at[3], halo_v, nxt)
    loads[1].wait()
    send("u1", up_all.at[h, s], up_all.at[h, s], sib)

    zero_row = jnp.zeros((40, 128), F32)
    zero_col = jnp.zeros((33, 8, 128), F32)
    for p in range(5):
        pf[p, 0] = zero_row
        pf[p, :, 0:8, :] = zero_col
    loads[0].wait()

    def widen(r, carry):
        for p in range(4):
            pf[p + 1, r + 1, 8:40, :] = vol_v[p, r].astype(F32)
        return carry

    lax.fori_loop(0, 32, widen, 0)

    def build(o, depth_taps):
        def step(n, carry):
            pi, ii = lax.div(n, 4), lax.rem(n, 4)
            for pj in range(2):
                base = pl.multiple_of((o * 4 + pi * 2 + pj) * 64 + ii * 16, 16)
                for a in depth_taps:
                    for b in range(3):
                        row = 8 * ii + 2 * pi + b
                        for c in range(3):
                            tap = 9 * a + 3 * b + c
                            cols = pl.ds(7 + 2 * pj + c, 8, stride=4)
                            both = [pf[2 * o + a, row + 4 * e, cols, :] for e in range(2)]
                            patch[pl.ds(base, 16), tap * 128 : (tap + 1) * 128] = jnp.concatenate(both, 0).astype(BF16)
            return carry

        lax.fori_loop(0, 8, step, 0)

    build(1, (0, 1, 2))
    got("u1")
    two = pl.ds(pair * 2, 2)
    send("u2", up_all.at[h, two], up_all.at[h, two], xpt)
    build(0, (1, 2))
    got("u2")
    four = pl.ds(y * 4, 4)
    send("u3", up_all.at[h, four], up_all.at[h, four], hpt)
    got("halo")

    def widen_halo(r, carry):
        pf[0, r + 1, 8:40, :] = jnp.where(s > 0, halo_v[r].astype(F32), 0.0)
        return carry

    lax.fori_loop(0, 32, widen_halo, 0)
    build(0, (0,))
    got("u3")
    send("u4p", up_all.at[:, four], up_all.at[:, four], yup)
    send("u4m", up_all.at[:, four], up_all.at[:, four], ydn)

    loads[2].wait()

    def conv_one(away):
        q = lax.rem(z + away, 4)

        def step(half, carry):
            rows = pl.ds(pl.multiple_of(half * 256, 256), 256)
            part[away, rows, :] = jnp.dot(patch[rows, :], k1_v[:, lanes(q)], preferred_element_type=F32)
            return carry

        lax.fori_loop(0, 2, step, 0)

    low, high = pl.ds(0, 256), pl.ds(256, 256)
    conv_one(2)
    send("m1p", part.at[2, low], mr1.at[0], zup)
    send("m1m", part.at[2, high], mr1.at[1], zdn)
    conv_one(1)
    send("m2pb", part.at[1, high], mr2.at[0, high], zup)
    conv_one(3)
    send("m2ma", part.at[3, low], mr2.at[1, low], zdn)
    got("m1p")
    part[1, 0:256] += mr1[0]
    send("m2pa", part.at[1, low], mr2.at[0, low], zup)
    got("m1m")
    part[3, 256:512] += mr1[1]
    send("m2mb", part.at[3, high], mr2.at[1, high], zdn)
    conv_one(0)

    got("u4p")
    got("u4m")
    below, above = pl.ds(ym * 4, 4), pl.ds(yp * 4, 4)
    send("u5p", up_all.at[0, below], up_all.at[0, below], yup)
    send("u5m", up_all.at[1, above], up_all.at[1, above], ydn)
    up_f[...] = jnp.zeros_like(up_f)
    for d in range(4):
        up_s[d, 1024:1088, :] = jnp.zeros((64, 256), BF16)
    got("u5p")
    got("u5m")

    def shifted(slab, carry):
        for half in range(2):
            up_f[0:8, 0:8, half * 128 : (half + 1) * 128] = up_all[half, slab].astype(F32).reshape(8, 8, 128)
        rows = pl.ds(pl.multiple_of(slab * 64, 64), 64)
        for di in range(2):
            for dj in range(2):
                up_s[di * 2 + dj, rows, :] = up_f[di : di + 8, dj : dj + 8, :].reshape(64, 256).astype(BF16)
        return carry

    lax.fori_loop(0, 16, shifted, 0)

    loads[3].wait()
    for phase in range(8):
        total = None
        for tap in range(27):
            if tap_phase(tap) != phase:
                continue
            do, di, dj = tap_shift(tap)
            rows = pl.ds(pl.multiple_of((s + do) * 64, 64), 64)
            term = lax.dot_general(
                up_s[di * 2 + dj, rows, :],
                k2_v[tap * 512 : (tap + 1) * 512, :],
                (((1,), (1,)), ((), ())),
                preferred_element_type=F32,
            )
            total = term if total is None else total + term
        for q in range(4):
            bpart[q, phase * 64 : (phase + 1) * 64, :] = total[:, q * 128 : (q + 1) * 128]
    bs1[...] = bpart[z2].astype(BF16)
    send("b1p", bs1.at[low], br1.at[0], zup)
    send("b1m", bs1.at[high], br1.at[1], zdn)
    bs2[0, 256:512] = bpart[zp, 256:512].astype(BF16)
    send("b2pb", bs2.at[0, high], br2.at[0, high], zup)
    bs2[1, 0:256] = bpart[zm, 0:256].astype(BF16)
    send("b2ma", bs2.at[1, low], br2.at[1, low], zdn)

    def turn(n, carry):
        flat = patch[:, pl.ds(pl.multiple_of(n * 256, 256), 256)].astype(F32).T
        rows = pl.ds(pl.multiple_of(n * 16, 16), 16)
        for owner in range(16):
            both = [flat[e * 128 + owner * 8 : e * 128 + owner * 8 + 8] for e in range(2)]
            patch_t[owner, rows, :] = jnp.concatenate(both, 0).astype(BF16)
        return carry

    lax.fori_loop(0, 13, turn, 0)
    flat = patch[:, 26 * 128 : 27 * 128].astype(F32).T
    for owner in range(16):
        both = [flat[owner * 8 : owner * 8 + 8], jnp.zeros((8, 512), F32)]
        patch_t[owner, 208:224, :] = jnp.concatenate(both, 0).astype(BF16)

    got("b1p")
    bs2[0, 0:256] = (bpart[zp, 0:256] + br1[0].astype(F32)).astype(BF16)
    send("b2pa", bs2.at[0, low], br2.at[0, low], zup)
    got("b1m")
    bs2[1, 256:512] = (bpart[zm, 256:512] + br1[1].astype(F32)).astype(BF16)
    send("b2mb", bs2.at[1, high], br2.at[1, high], zdn)

    for name in ("m2pb", "m2ma", "m2pa", "m2mb"):
        got(name)
    mixed = part[0] + mr2[0] + mr2[1]
    part[0] = mixed
    hid[:, lanes(z)] = jnp.where(mixed > 0, mixed, SLOPE * mixed).astype(BF16)
    send("h1p", hid.at[:, lanes(z)], hid.at[:, lanes(z)], zup)
    send("h1m", hid.at[:, lanes(z)], hid.at[:, lanes(z)], zdn)
    for name in ("b2pb", "b2ma", "b2pa", "b2mb"):
        got(name)
    back = bpart[z] + br2[0].astype(F32) + br2[1].astype(F32)
    dlt[:, lanes(z)] = (back * jnp.where(part[0] > 0, 1.0, SLOPE)).astype(BF16)
    send("d1p", dlt.at[:, lanes(z)], dlt.at[:, lanes(z)], zup)
    send("d1m", dlt.at[:, lanes(z)], dlt.at[:, lanes(z)], zdn)

    def grad_one(slot):
        q = lax.rem(z + slot, 4)

        def away(n, carry):
            rows = pl.ds(pl.multiple_of(lax.rem(n, 2) * 224, 32), 224)
            term = jnp.dot(patch_t[2 * n + 1 - k], dlt[:, lanes(q)], preferred_element_type=F32)
            ksend[slot, lax.div(n, 2), rows, :] = term.astype(BF16)
            return carry

        def kept(n, carry):
            rows = pl.ds(pl.multiple_of(lax.rem(n, 2) * 224, 32), 224)
            term = jnp.dot(patch_t[2 * n + k], dlt[:, lanes(q)], preferred_element_type=F32)
            acc[slot, lax.div(n, 2), rows, :] = term
            return carry

        lax.fori_loop(0, 8, away, 0)
        send(f"k{slot}", ksend.at[slot], krecv.at[slot], sib)
        lax.fori_loop(0, 8, kept, 0)

    def add_sibling(slot):
        got(f"k{slot}")

        def step(n, carry):
            acc[slot, n] += krecv[slot, n].astype(F32)
            return carry

        lax.fori_loop(0, 4, step, 0)

    def y_first(slot, ref, rows):
        half = rows // 2
        ys1[slot, 0:rows] = ref[y2].astype(BF16)
        send(f"p{slot}", ys1.at[slot, 0:half], yr1.at[slot, 0, 0:half], yup)
        send(f"q{slot}", ys1.at[slot, half:rows], yr1.at[slot, 1, 0:half], ydn)

    def y_second(slot, ref, rows):
        half = rows // 2
        got(f"p{slot}")
        ys2[slot, 0, 0:half] = (ref[yp, 0:half] + yr1[slot, 0, 0:half].astype(F32)).astype(BF16)
        ys2[slot, 0, half:rows] = ref[yp, half:rows].astype(BF16)
        send(f"r{slot}", ys2.at[slot, 0, 0:rows], yr2.at[slot, 0, 0:rows], yup)
        got(f"q{slot}")
        ys2[slot, 1, 0:half] = ref[ym, 0:half].astype(BF16)
        ys2[slot, 1, half:rows] = (ref[ym, half:rows] + yr1[slot, 1, 0:half].astype(F32)).astype(BF16)
        send(f"t{slot}", ys2.at[slot, 1, 0:rows], yr2.at[slot, 1, 0:rows], ydn)

    def y_third(slot, ref, rows):
        got(f"r{slot}")
        got(f"t{slot}")
        ref[y, 0:rows] = ref[y, 0:rows] + yr2[slot, 0, 0:rows].astype(F32) + yr2[slot, 1, 0:rows].astype(F32)

    mine = pl.ds(pl.multiple_of(xl * 224, 32), 224)
    other = pl.ds(pl.multiple_of((1 - xl) * 224, 32), 224)

    def put_grad_one(slot, value):
        q = lax.rem(z + slot, 4)
        g1_o[:, :, lanes(q)] = value[0:216].reshape(27, 8, 128)

    def x_first(slot, lane):
        for n in range(4):
            xs4[lane, n] = acc[slot, n, other].astype(BF16)
        send(f"x{slot}", xs4.at[lane], xr4.at[lane], xpt)

    def x_second(slot, lane):
        got(f"x{slot}")
        for n in range(4):
            accx[lane, n] = acc[slot, n, mine] + xr4[lane, n].astype(F32)

    def x_last(slot, lane):
        xs1[lane] = acc[slot, y, other].astype(BF16)
        send(f"x{slot}", xs1.at[lane], xr1.at[lane], xpt)

    def x_done(slot, lane):
        got(f"x{slot}")
        put_grad_one(slot, acc[slot, y, mine] + xr1[lane].astype(F32))

    zm_rows, zp_rows = low, high

    grad_one(0)
    got("h1p")
    send("h2p", hid.at[zm_rows, lanes(zm)], hid.at[zm_rows, lanes(zm)], zup)
    got("h1m")
    send("h2m", hid.at[zp_rows, lanes(zp)], hid.at[zp_rows, lanes(zp)], zdn)
    add_sibling(0)
    y_first(0, acc.at[0], 448)
    got("d1p")
    send("d2p", dlt.at[zm_rows, lanes(zm)], dlt.at[zm_rows, lanes(zm)], zup)
    got("d1m")
    send("d2m", dlt.at[zp_rows, lanes(zp)], dlt.at[zp_rows, lanes(zp)], zdn)
    grad_one(1)
    add_sibling(1)
    x_first(1, 0)
    y_second(0, acc.at[0], 448)
    grad_one(3)
    add_sibling(3)
    x_first(3, 1)
    got("h2p")
    got("h2m")

    def turn_hidden(q, carry):
        flat = hid[:, lanes(q)].astype(F32).T.astype(BF16)
        for xd in range(2):
            for kd in range(2):
                j = xd * 2 + kd
                gh[kd, xd, q, xl * 2 + k] = flat[j * 32 : (j + 1) * 32]
        return carry

    lax.fori_loop(0, 4, turn_hidden, 0)
    src = xl * 2 + k
    send("g1", gh.at[1 - k, :, :, src], gh.at[1 - k, :, :, src], sib)
    x_second(1, 0)
    y_first(1, accx.at[0], 224)
    got("d2p")
    got("d2m")
    grad_one(2)
    y_third(0, acc.at[0], 448)
    x_last(0, 0)
    got("g1")
    pair_src = pl.ds(xl * 2, 2)
    send("g2", gh.at[k, 1 - xl, :, pair_src], gh.at[k, 1 - xl, :, pair_src], xpt)
    add_sibling(2)
    y_first(2, acc.at[2], 448)
    x_second(3, 1)
    y_first(3, accx.at[1], 224)
    y_second(1, accx.at[0], 224)

    fs[...] = jnp.zeros_like(fs)
    for later in range(2):
        for d in range(4):
            total = None
            for tap in range(27):
                do, di, dj = tap_shift(tap)
                if do != later or di * 2 + dj != d:
                    continue
                phase = tap_phase(tap)
                term = jnp.dot(
                    hid[phase * 64 : (phase + 1) * 64, :],
                    k2_v[tap * 512 : (tap + 1) * 512, :],
                    preferred_element_type=F32,
                )
                total = term if total is None else total + term
            fs[later, d, 1:9, 8:16, :] = total.reshape(8, 8, 256)
    for later in range(2):
        total = None
        for d in range(4):
            di, dj = d // 2, d % 2
            term = fs[later, d, 1 - di : 9 - di, 8 - dj : 16 - dj, :]
            total = term if total is None else total + term
        fp[later] = total.reshape(64, 256)
    send("f1", fp.at[1], fr, nxt)

    got("g2")
    hh[y] = gh[k, xl, y]
    send("g3p", gh.at[k, xl, yp], hh.at[y], yup)
    send("g3m", gh.at[k, xl, ym], hh.at[y], ydn)
    send("g3f", gh.at[k, xl, y2], hh.at[y], yfar)
    y_second(2, acc.at[2], 448)
    y_second(3, accx.at[1], 224)

    got("f1")
    whole = fp[0] + jnp.where(s > 0, fr[...], 0.0)
    for half in range(2):
        fx[half] = whole[:, half * 128 : (half + 1) * 128]
    send("f2", fx.at[1 - h], fxr, hpt)

    y_third(1, accx.at[0], 224)
    put_grad_one(1, accx[0, y])
    x_done(0, 0)

    got("g3p")
    got("g3m")
    got("g3f")
    for phase in range(8):
        for m in range(8):
            two_slabs = [hh[(2 * m + e) // 4, (2 * m + e) % 4, :, phase * 64 : (phase + 1) * 64] for e in range(2)]
            hp[phase * 32 : (phase + 1) * 32, m * 128 : (m + 1) * 128] = jnp.concatenate(two_slabs, 1)
    for do in range(2):
        for d in range(4):
            di, dj = d // 2, d % 2
            grads = jnp.dot(hp[...], up_s[d, do * 64 : do * 64 + 1024, :], preferred_element_type=F32)
            for tap in range(27):
                if tap_shift(tap) == (do, di, dj):
                    phase = tap_phase(tap)
                    g2_o[tap] = grads[phase * 32 : (phase + 1) * 32]

    y_third(2, acc.at[2], 448)
    x_last(2, 1)
    y_third(3, accx.at[1], 224)
    put_grad_one(3, accx[1, y])
    got("f2")
    feat_o[...] = fx[h] + fxr[...]
    x_done(2, 1)
    for message in msgs.values():
        message.wait_send()


def local(volume, kernel_one, kernel_two, upstream):
    any_spec = pl.BlockSpec(memory_space=pl.ANY)
    vmem_spec = pl.BlockSpec(memory_space=pltpu.VMEM)
    v = pltpu.VMEM
    feat, g1, g2 = pl.pallas_call(
        body,
        out_shape=(
            jax.ShapeDtypeStruct((64, 128), F32),
            jax.ShapeDtypeStruct((27, 8, 512), F32),
            jax.ShapeDtypeStruct((27, 32, 256), F32),
        ),
        in_specs=[any_spec] * 4,
        out_specs=(vmem_spec,) * 3,
        scratch_shapes=[
            v((4, 32, 32, 128), BF16),
            v((32, 32, 128), BF16),
            v((3456, 512), BF16),
            v((27 * 512, 256), BF16),
            v((5, 33, 40, 128), F32),
            v((512, 3456), BF16),
            v((16, 224, 512), BF16),
            v((2, 16, 64, 128), BF16),
            v((9, 16, 256), F32),
            v((4, 1088, 256), BF16),
            v((4, 512, 128), F32),
            v((2, 256, 128), F32),
            v((2, 512, 128), F32),
            v((4, 512, 128), F32),
            v((512, 128), BF16),
            v((2, 512, 128), BF16),
            v((2, 256, 128), BF16),
            v((2, 512, 128), BF16),
            v((512, 512), BF16),
            v((512, 512), BF16),
            v((4, 4, 448, 128), F32),
            v((4, 4, 448, 128), BF16),
            v((4, 4, 448, 128), BF16),
            v((2, 4, 224, 128), F32),
            v((2, 4, 224, 128), BF16),
            v((2, 4, 224, 128), BF16),
            v((2, 224, 128), BF16),
            v((2, 224, 128), BF16),
            v((4, 448, 128), BF16),
            v((4, 2, 224, 128), BF16),
            v((4, 2, 448, 128), BF16),
            v((4, 2, 448, 128), BF16),
            v((2, 2, 4, 4, 32, 512), BF16),
            v((4, 4, 32, 512), BF16),
            v((256, 1024), BF16),
            v((2, 4, 9, 16, 256), F32),
            v((2, 64, 256), F32),
            v((64, 256), F32),
            v((2, 64, 128), F32),
            v((64, 128), F32),
            pltpu.SemaphoreType.DMA((4,)),
            pltpu.SemaphoreType.DMA((NMSG,)),
            pltpu.SemaphoreType.DMA((NMSG,)),
        ],
        compiler_params=pltpu.CompilerParams(
            collective_id=0, has_side_effects=True, vmem_limit_bytes=60 * 1024 * 1024
        ),
        cost_estimate=pl.CostEstimate(flops=6_000_000_000, bytes_accessed=14_000_000, transcendentals=0),
        name="two_layers",
    )(
        volume,
        kernel_one.reshape(27 * 128, 512),
        kernel_two.reshape(27 * 512, 256),
        upstream.reshape(64, 128),
    )
    return feat.reshape(1, 8, 8, 128), g1, g2


def solution(mesh):
    return jax.shard_map(
        local,
        mesh=mesh,
        in_specs=(
            P("space", None, None, "chan"),
            P(None, "chan", "filt"),
            P(None, "filt", "chan"),
            P("space", None, None, ("chan", "filt")),
        ),
        out_specs=(
            P("space", None, None, ("chan", "filt")),
            P(None, ("chan", "space"), "filt"),
            P(None, ("filt", "space"), "chan"),
        ),
        check_vma=False,
    )
```

time: 460 us -> 88.1 us (0.19); the launches traced: 452 us -> 87.8 us
  waiting for transfers between devices: 304 us -> 0 us
  Pallas kernels: 0 us -> 81.8 us
  local copies, waits for them, and re-layouts: 79.4 us -> 5.35 us
  matrix products: 29.5 us -> 0 us
  between operations: 14.8 us -> 0.64 us
  other arithmetic: 9.8 us -> 0 us
  starting transfers between devices: 7.7 us -> 0 us
  blocking collectives: 6.28 us -> 0 us
    reduce_scatter x3 -> x0, waiting for transfers between devices: 243 us -> none  [the longest x1 158 us: local(): lax.psum_scatter(term_two, 'space', scatter_dimension=1, tiled=True)]
    pallas_call x0 -> x1, Pallas kernels: none -> 81.8 us  [local(): pl.pallas_call(body, out_shape=(jax.ShapeDtypeStruct((64, 128), F32), jax...]
    psum x1 -> x0, waiting for transfers between devices: 61.6 us -> none  [local(): mixed_sum = lax.psum(partial_value, 'chan')]
    dot_general x5 -> x0, matrix products: 29.5 us -> none  [the longest x1 8.59 us: local(): lax.dot_general(patch_two, seed_block.reshape(-1, out_local), (((0,), (0,...]
    reshape x4 -> x0, local copies, waits for them, and re-layouts: 28.7 us -> none  [the longest x1 18.2 us: spread(): jnp.transpose(stacked, (3, 0, 4, 1, 5, 2, 6))]
    slice x8 -> x0, local copies, waits for them, and re-layouts: 20.4 us -> none  [the longest x4 14.8 us: patches(): phases[depth_tap // 2:depth_tap // 2 + depth_out, depth_tap % 2, row_tap...]
    ppermute x3 -> x0, starting transfers between devices: 7.54 us -> none  [passed_along(): return lax.ppermute(block, axis, route)]
    all_gather x1 -> x0, blocking collectives: 6.28 us -> none  [local(): seed_block = lax.all_gather(upstream, 'filt', axis=3, tiled=True)]
  transfers between devices with their start and end apart: 7 -> 0, of which waited for: 3 -> 0; matrix products, arithmetic and copies ran while one was open for 15% -> 0% of each run, Pallas kernels for 0% -> 0%
where the time goes in v1:
time: 88.1 us; the launch traced here: 87.8 us
  Pallas kernels  81.8 us (93%)
  local copies, waits for them, and re-layouts  5.35 us (6%)
    pallas_call x1, Pallas kernels, local(): pl.pallas_call(body, out_shape=(jax.ShapeDtypeStruct((64, 128), F32), jax...  81.8 us
    unnamed x3, local copies, waits for them, and re-layouts  5.35 us

profile of v1, /device:TPU:0, one launch (start us, length us, event | category | flops | bytes accessed | tf_op | source)
XLA Modules:
  0.0 87.8 jit_solution(13993885846070975067)
XLA Ops:
  0.6 81.8 %two_layers.1 = (f32[64,128]{1,0:T(8,128)}, f32[27,8,512]{2,1,0:T(8,128)}, f32[27,32,256]{2,1,0:T(8,128)}) custom-call(bf16[4,32,32,128]{3,2,1,0:T(8,128)(2,1)} %vol.1, bf16[3456,512]{1,0:T(8,128)(2,1)} %bitcast.6, bf16[13824,256]{1,0:T(8,128)(2,1)} %bitcast.5, bf16[64,128]{1,0:T(8,128)(2,1)} %bitcast.7), custom_call_target="tpu_custom_call" | custom-call | flops 6000000000 | bytes 14000000 | tf_op jit(solution)/shard_map/two_layers/pallas_call | solution.py:443
  82.5 1.4 %copy.10 = f32[1,8,8,128]{3,2,1,0:T(8,128)} copy(f32[1,8,8,128]{3,2,1,0:T(8,128)} %bitcast.4) | data formatting | bytes 65536
  83.8 1.8 %copy.11 = f32[27,8,512]{2,1,0:T(8,128)} copy(f32[27,8,512]{2,1,0:T(8,128)} %get-tuple-element.13) | data formatting | bytes 884736
  85.6 2.2 %copy.12 = f32[27,32,256]{2,1,0:T(8,128)} copy(f32[27,32,256]{2,1,0:T(8,128)} %get-tuple-element.14) | data formatting | bytes 1769472

commit v2 on v1

v2 whole, which is shorter than its diff:
```python
import jax
import jax.numpy as jnp
from jax import lax
from jax.experimental import pallas as pl
from jax.experimental.pallas import tpu as pltpu
from jax.sharding import PartitionSpec as P

SLOPE = 0.3
F32, BF16 = jnp.float32, jnp.bfloat16
MESH = pl.DeviceIdType.MESH
NMSG = 80


def tap_parts(tap):
    return tap // 9, (tap // 3) % 3, tap % 3


def tap_phase(tap):
    a, b, c = tap_parts(tap)
    return ((a != 1) * 2 + (b != 1)) * 2 + (c != 1)


def tap_shift(tap):
    return tuple(int(v == 0) for v in tap_parts(tap))


def body(
    vol, k1, k2, up, feat_o, g1_o, g2_o,
    vol_v, halo_v, k1_v, k2_v, pf, patch, patch_t,
    up_all, up_next, up_f, up_s, seed_s,
    part, mr1, mr2, bpart, bs1, bs2, br1, br2,
    hid, dlt,
    acc, ksend, krecv, accx, xs4, xr4, xs1, xr1, ys1, yr1, ys2, yr2,
    gh, hh, hp, fs, fp, fr, fx, fxr, feat_v, g1_v, g2_v,
    lsem, ssem, rsem,
):
    s, z, h = lax.axis_index("space"), lax.axis_index("chan"), lax.axis_index("filt")
    k, pair = lax.rem(s, 2), lax.div(s, 2)
    xl, y = lax.rem(pair, 2), lax.div(pair, 2)
    zp, zm, z2 = lax.rem(z + 1, 4), lax.rem(z + 3, 4), lax.rem(z + 2, 4)
    yp, ym, y2 = lax.rem(y + 1, 4), lax.rem(y + 3, 4), lax.rem(y + 2, 4)
    around = [lax.rem(s + d, 16) for d in range(16)]
    sib = {"space": s + 1 - 2 * k}
    xpt = {"space": y * 4 + (1 - xl) * 2 + k}
    hpt = {"filt": 1 - h}
    yup, ydn, yfar = ({"space": v * 4 + xl * 2 + k} for v in (yp, ym, y2))
    zup, zdn, zfar = {"chan": zp}, {"chan": zm}, {"chan": z2}
    nxt, prv = {"space": around[1]}, {"space": around[15]}
    nxt_h, prv_h = {"space": around[1], "filt": 1 - h}, {"space": around[15], "filt": 1 - h}

    msgs = {}

    def send(name, src, dst, device):
        i = len(msgs)
        msgs[name] = pltpu.make_async_remote_copy(
            src_ref=src, dst_ref=dst, send_sem=ssem.at[i], recv_sem=rsem.at[i], device_id=device, device_id_type=MESH
        )
        msgs[name].start()

    def got(name):
        msgs[name].wait_recv()

    def lanes(q):
        return pl.ds(pl.multiple_of(q * 128, 128), 128)

    loads = [
        pltpu.make_async_copy(vol, vol_v, lsem.at[0]),
        pltpu.make_async_copy(up, up_all.at[h, s], lsem.at[1]),
        pltpu.make_async_copy(k1, k1_v, lsem.at[2]),
        pltpu.make_async_copy(k2, k2_v, lsem.at[3]),
    ]
    for copy in loads:
        copy.start()

    barrier = pltpu.get_barrier_semaphore()
    greeted = [{"space": v} for v in around[1:]] + [zup, zdn, zfar, hpt, nxt_h, prv_h]
    for device in greeted:
        pl.semaphore_signal(barrier, inc=1, device_id=device, device_id_type=MESH)
    pl.semaphore_wait(barrier, len(greeted))

    send("halo", vol.at[3], halo_v, nxt)
    loads[1].wait()
    send("u0", up_all.at[h, s], up_all.at[h, s], hpt)
    send("u1", up_all.at[h, s], up_next.at[h], prv)
    send("u2", up_all.at[h, s], up_next.at[h], prv_h)

    zero_row = jnp.zeros((40, 128), F32)
    zero_col = jnp.zeros((33, 8, 128), F32)
    for p in range(5):
        pf[p, 0] = zero_row
        pf[p, :, 0:8, :] = zero_col
    loads[0].wait()

    def widen(r, carry):
        for p in range(4):
            pf[p + 1, r + 1, 8:40, :] = vol_v[p, r].astype(F32)
        return carry

    lax.fori_loop(0, 32, widen, 0)

    def build(o, depth_taps):
        def step(n, carry):
            pi, ii = lax.div(n, 4), lax.rem(n, 4)
            for pj in range(2):
                base = pl.multiple_of((o * 4 + pi * 2 + pj) * 64 + ii * 16, 16)
                for a in depth_taps:
                    for b in range(3):
                        row = 8 * ii + 2 * pi + b
                        for c in range(3):
                            tap = 9 * a + 3 * b + c
                            cols = pl.ds(7 + 2 * pj + c, 8, stride=4)
                            both = [pf[2 * o + a, row + 4 * e, cols, :] for e in range(2)]
                            patch[pl.ds(base, 16), tap * 128 : (tap + 1) * 128] = jnp.concatenate(both, 0).astype(BF16)
            return carry

        lax.fori_loop(0, 8, step, 0)

    build(1, (0, 1, 2))
    loads[2].wait()
    low, high = pl.ds(0, 256), pl.ds(256, 256)

    def conv_one(first, second, rows):
        weights = jnp.concatenate([k1_v[:, lanes(lax.rem(z + away, 4))] for away in (first, second)], 1)
        both = jnp.dot(patch[rows, :], weights, preferred_element_type=F32)
        part[first, rows, :] = both[:, 0:128]
        part[second, rows, :] = both[:, 128:256]

    conv_one(2, 1, high)
    send("m1m", part.at[2, high], mr1.at[1], zdn)
    send("m2pb", part.at[1, high], mr2.at[0, high], zup)
    conv_one(3, 0, high)

    up_f[...] = jnp.zeros_like(up_f)

    def moved(blocks, store):
        for half in range(2):
            up_f[0:8, 0:8, half * 128 : (half + 1) * 128] = blocks[half].astype(F32).reshape(8, 8, 128)
        for di in range(2):
            for dj in range(2):
                store(di * 2 + dj, up_f[di : di + 8, dj : dj + 8, :].reshape(64, 256).astype(BF16))

    got("u0")
    got("u1")
    got("u2")
    own_pair = up_all.at[:, s]
    for d in range(1, 16):
        send(f"a{d}", own_pair, own_pair, {"space": around[d]})

    def store_seed(later):
        def store(d, value):
            seed_s[later, d] = value

        return store

    moved([up_all[half, s] for half in range(2)], store_seed(0))
    moved([jnp.where(s < 15, up_next[half].astype(F32), 0.0) for half in range(2)], store_seed(1))

    loads[3].wait()
    for phase in range(8):
        total = None
        for tap in range(27):
            if tap_phase(tap) != phase:
                continue
            do, di, dj = tap_shift(tap)
            term = lax.dot_general(
                seed_s[do, di * 2 + dj],
                k2_v[tap * 512 : (tap + 1) * 512, :],
                (((1,), (1,)), ((), ())),
                preferred_element_type=F32,
            )
            total = term if total is None else total + term
        for q in range(4):
            bpart[q, phase * 64 : (phase + 1) * 64, :] = total[:, q * 128 : (q + 1) * 128]
    bs1[...] = bpart[z2].astype(BF16)
    send("b1p", bs1.at[low], br1.at[0], zup)
    send("b1m", bs1.at[high], br1.at[1], zdn)
    bs2[0, 256:512] = bpart[zp, 256:512].astype(BF16)
    send("b2pb", bs2.at[0, high], br2.at[0, high], zup)
    bs2[1, 0:256] = bpart[zm, 0:256].astype(BF16)
    send("b2ma", bs2.at[1, low], br2.at[1, low], zdn)

    build(0, (1, 2))
    got("halo")

    def widen_halo(r, carry):
        pf[0, r + 1, 8:40, :] = jnp.where(s > 0, halo_v[r].astype(F32), 0.0)
        return carry

    lax.fori_loop(0, 32, widen_halo, 0)
    build(0, (0,))
    conv_one(2, 3, low)
    send("m1p", part.at[2, low], mr1.at[0], zup)
    send("m2ma", part.at[3, low], mr2.at[1, low], zdn)
    got("m1m")
    part[3, 256:512] += mr1[1]
    send("m2mb", part.at[3, high], mr2.at[1, high], zdn)
    conv_one(1, 0, low)
    got("m1p")
    part[1, 0:256] += mr1[0]
    send("m2pa", part.at[1, low], mr2.at[0, low], zup)
    got("b1p")
    bs2[0, 0:256] = (bpart[zp, 0:256] + br1[0].astype(F32)).astype(BF16)
    send("b2pa", bs2.at[0, low], br2.at[0, low], zup)
    got("b1m")
    bs2[1, 256:512] = (bpart[zm, 256:512] + br1[1].astype(F32)).astype(BF16)
    send("b2mb", bs2.at[1, high], br2.at[1, high], zdn)

    def put_turned(flat_rows, rows_at):
        for owner in range(16):
            yd, xd, kd = owner // 4, (owner // 2) % 2, owner % 2
            patch_t[kd, yd, pl.ds(pl.multiple_of(rows_at + xd * 224, 16), 16), :] = flat_rows(owner).astype(BF16)

    def turn(n, carry):
        flat = patch[:, pl.ds(pl.multiple_of(n * 256, 256), 256)].astype(F32).T

        def two_taps(owner):
            return jnp.concatenate([flat[e * 128 + owner * 8 : e * 128 + owner * 8 + 8] for e in range(2)], 0)

        put_turned(two_taps, n * 16)
        return carry

    lax.fori_loop(0, 13, turn, 0)
    flat = patch[:, 26 * 128 : 27 * 128].astype(F32).T
    put_turned(lambda owner: jnp.concatenate([flat[owner * 8 : owner * 8 + 8], jnp.zeros((8, 512), F32)], 0), 208)

    for d in range(4):
        up_s[d, 1024:1088, :] = jnp.zeros((64, 256), BF16)
    for d in range(1, 16):
        got(f"a{d}")

    def shifted(slab, carry):
        def store(d, value):
            up_s[d, pl.ds(pl.multiple_of(slab * 64, 64), 64), :] = value

        moved([up_all[half, slab] for half in range(2)], store)
        return carry

    lax.fori_loop(0, 16, shifted, 0)

    for name in ("m2pb", "m2ma", "m2pa", "m2mb"):
        got(name)
    mixed = part[0] + mr2[0] + mr2[1]
    part[0] = mixed
    hid[:, lanes(z)] = jnp.where(mixed > 0, mixed, SLOPE * mixed).astype(BF16)
    for name in ("b2pb", "b2ma", "b2pa", "b2mb"):
        got(name)
    back = bpart[z] + br2[0].astype(F32) + br2[1].astype(F32)
    dlt[:, lanes(z)] = (back * jnp.where(part[0] > 0, 1.0, SLOPE)).astype(BF16)
    for tag, ref in (("d", dlt), ("h", hid)):
        for way, device in (("p", zup), ("m", zdn), ("f", zfar)):
            send(tag + way, ref.at[:, lanes(z)], ref.at[:, lanes(z)], device)

    def grad_one(slots):
        deltas = jnp.concatenate([dlt[:, lanes(lax.rem(z + slot, 4))] for slot in slots], 1)
        for yd in range(4):
            term = jnp.dot(patch_t[1 - k, yd], deltas, preferred_element_type=F32)
            for i, slot in enumerate(slots):
                ksend[slot, yd] = term[:, i * 128 : (i + 1) * 128].astype(BF16)
        for slot in slots:
            send(f"k{slot}", ksend.at[slot], krecv.at[slot], sib)
        for yd in range(4):
            term = jnp.dot(patch_t[k, yd], deltas, preferred_element_type=F32)
            for i, slot in enumerate(slots):
                acc[slot, yd] = term[:, i * 128 : (i + 1) * 128]

    def add_sibling(slot):
        got(f"k{slot}")

        def step(n, carry):
            acc[slot, n] += krecv[slot, n].astype(F32)
            return carry

        lax.fori_loop(0, 4, step, 0)

    def ring_first(slot, ref, rows):
        half = rows // 2
        ys1[0:rows] = ref[y2].astype(BF16)
        send(f"p{slot}", ys1.at[0:half], yr1.at[0, 0:half], yup)
        send(f"q{slot}", ys1.at[half:rows], yr1.at[1, 0:half], ydn)

    def ring_second(slot, ref, rows):
        half = rows // 2
        got(f"p{slot}")
        ys2[slot, 0, 0:half] = (ref[yp, 0:half] + yr1[0, 0:half].astype(F32)).astype(BF16)
        ys2[slot, 0, half:rows] = ref[yp, half:rows].astype(BF16)
        send(f"r{slot}", ys2.at[slot, 0, 0:rows], yr2.at[slot, 0, 0:rows], yup)
        got(f"q{slot}")
        ys2[slot, 1, 0:half] = ref[ym, 0:half].astype(BF16)
        ys2[slot, 1, half:rows] = (ref[ym, half:rows] + yr1[1, 0:half].astype(F32)).astype(BF16)
        send(f"t{slot}", ys2.at[slot, 1, 0:rows], yr2.at[slot, 1, 0:rows], ydn)

    def ring_third(slot, ref, rows):
        got(f"r{slot}")
        got(f"t{slot}")
        ref[y, 0:rows] = ref[y, 0:rows] + yr2[slot, 0, 0:rows].astype(F32) + yr2[slot, 1, 0:rows].astype(F32)

    def straight(slot, ref, rows):
        for i, (v, device) in enumerate(((y2, yfar), (yp, yup), (ym, ydn))):
            ys2[slot, i, 0:rows] = ref[v].astype(BF16)
            send(f"y{slot}{i}", ys2.at[slot, i, 0:rows], yr2.at[slot, i, 0:rows], device)

    def straight_sum(slot, ref, rows):
        for i in (1, 2, 0):
            got(f"y{slot}{i}")
        total = ref[y, 0:rows]
        for i in range(3):
            total = total + yr2[slot, i, 0:rows].astype(F32)
        ref[y, 0:rows] = total

    mine = pl.ds(pl.multiple_of(xl * 224, 32), 224)
    other = pl.ds(pl.multiple_of((1 - xl) * 224, 32), 224)

    def put_grad_one(slot, value):
        q = lax.rem(z + slot, 4)
        g1_v[:, :, lanes(q)] = value[0:216].reshape(27, 8, 128)

    def x_first(slot, lane):
        for n in range(4):
            xs4[lane, n] = acc[slot, n, other].astype(BF16)
        send(f"x{slot}", xs4.at[lane], xr4.at[lane], xpt)

    def x_second(slot, lane):
        got(f"x{slot}")
        for n in range(4):
            accx[lane, n] = acc[slot, n, mine] + xr4[lane, n].astype(F32)

    def x_last(slot, lane):
        xs1[lane] = acc[slot, y, other].astype(BF16)
        send(f"x{slot}", xs1.at[lane], xr1.at[lane], xpt)

    def x_done(slot, lane):
        got(f"x{slot}")
        put_grad_one(slot, acc[slot, y, mine] + xr1[lane].astype(F32))

    grad_one((0,))
    add_sibling(0)
    ring_first(0, acc.at[0], 448)
    got("dp")
    got("dm")
    grad_one((1, 3))
    ring_second(0, acc.at[0], 448)
    add_sibling(1)
    x_first(1, 0)
    add_sibling(3)
    x_first(3, 1)
    got("df")
    grad_one((2,))
    add_sibling(2)
    straight(2, acc.at[2], 448)
    ring_third(0, acc.at[0], 448)
    x_last(0, 0)
    x_second(1, 0)
    straight(1, accx.at[0], 224)
    x_second(3, 1)
    straight(3, accx.at[1], 224)
    for way in "pmf":
        got("h" + way)

    def turn_hidden(q, carry):
        flat = hid[:, lanes(q)].astype(F32).T.astype(BF16)
        for j in range(4):
            gh[q * 4 + j] = flat[j * 32 : (j + 1) * 32]
        return carry

    lax.fori_loop(0, 4, turn_hidden, 0)
    for d in range(1, 16):
        send(f"g{d}", gh.at[around[d]], hh.at[s], {"space": around[d]})
    hh[s] = gh[s]

    fs[...] = jnp.zeros_like(fs)
    for later in range(2):
        for d in range(4):
            total = None
            for tap in range(27):
                do, di, dj = tap_shift(tap)
                if do != later or di * 2 + dj != d:
                    continue
                phase = tap_phase(tap)
                term = jnp.dot(
                    hid[phase * 64 : (phase + 1) * 64, :],
                    k2_v[tap * 512 : (tap + 1) * 512, :],
                    preferred_element_type=F32,
                )
                total = term if total is None else total + term
            fs[later, d, 1:9, 8:16, :] = total.reshape(8, 8, 256)
    for later in range(2):
        total = None
        for d in range(4):
            di, dj = d // 2, d % 2
            term = fs[later, d, 1 - di : 9 - di, 8 - dj : 16 - dj, :]
            total = term if total is None else total + term
        fp[later] = total.reshape(64, 256)
    send("f1", fp.at[1], fr, nxt)

    straight_sum(2, acc.at[2], 448)
    x_last(2, 1)
    got("f1")
    whole = fp[0] + jnp.where(s > 0, fr[...], 0.0)
    for half in range(2):
        fx[half] = whole[:, half * 128 : (half + 1) * 128]
    send("f2", fx.at[1 - h], fxr, hpt)
    straight_sum(1, accx.at[0], 224)
    put_grad_one(1, accx[0, y])
    straight_sum(3, accx.at[1], 224)
    put_grad_one(3, accx[1, y])
    x_done(0, 0)

    for d in range(1, 16):
        got(f"g{d}")
    for phase in range(8):
        for m in range(8):
            two_slabs = [hh[2 * m + e, :, phase * 64 : (phase + 1) * 64] for e in range(2)]
            hp[phase * 32 : (phase + 1) * 32, m * 128 : (m + 1) * 128] = jnp.concatenate(two_slabs, 1)
    for do in range(2):
        for d in range(4):
            di, dj = d // 2, d % 2
            grads = jnp.dot(hp[...], up_s[d, do * 64 : do * 64 + 1024, :], preferred_element_type=F32)
            for tap in range(27):
                if tap_shift(tap) == (do, di, dj):
                    phase = tap_phase(tap)
                    g2_v[tap] = grads[phase * 32 : (phase + 1) * 32]
    stores = [pltpu.make_async_copy(g2_v, g2_o, lsem.at[4])]
    stores[0].start()
    x_done(2, 1)
    stores.append(pltpu.make_async_copy(g1_v, g1_o, lsem.at[5]))
    stores[1].start()
    got("f2")
    feat_v[...] = fx[h] + fxr[...]
    stores.append(pltpu.make_async_copy(feat_v, feat_o, lsem.at[6]))
    stores[2].start()
    for message in msgs.values():
        message.wait_send()
    for copy in stores:
        copy.wait()


def place(feat, g1, g2, feat_o, g1_o, g2_o):
    feat_o[...] = feat[...]
    g1_o[...] = g1[...]
    g2_o[...] = g2[...]


def local(volume, kernel_one, kernel_two, upstream):
    any_spec = pl.BlockSpec(memory_space=pl.ANY)
    v = pltpu.VMEM
    shapes = (
        jax.ShapeDtypeStruct((64, 128), F32),
        jax.ShapeDtypeStruct((27, 8, 512), F32),
        jax.ShapeDtypeStruct((27, 32, 256), F32),
    )
    place_specs = (
        pl.BlockSpec((64, 128), lambda i: (0, 0)),
        pl.BlockSpec((9, 8, 512), lambda i: (i, 0, 0)),
        pl.BlockSpec((9, 32, 256), lambda i: (i, 0, 0)),
    )
    results = pl.pallas_call(
        body,
        out_shape=shapes,
        in_specs=[any_spec] * 4,
        out_specs=(any_spec,) * 3,
        scratch_shapes=[
            v((4, 32, 32, 128), BF16),
            v((32, 32, 128), BF16),
            v((3456, 512), BF16),
            v((27 * 512, 256), BF16),
            v((5, 33, 40, 128), F32),
            v((512, 3456), BF16),
            v((2, 4, 448, 512), BF16),
            v((2, 16, 64, 128), BF16),
            v((2, 64, 128), BF16),
            v((9, 16, 256), F32),
            v((4, 1088, 256), BF16),
            v((2, 4, 64, 256), BF16),
            v((4, 512, 128), F32),
            v((2, 256, 128), F32),
            v((2, 512, 128), F32),
            v((4, 512, 128), F32),
            v((512, 128), BF16),
            v((2, 512, 128), BF16),
            v((2, 256, 128), BF16),
            v((2, 512, 128), BF16),
            v((512, 512), BF16),
            v((512, 512), BF16),
            v((4, 4, 448, 128), F32),
            v((4, 4, 448, 128), BF16),
            v((4, 4, 448, 128), BF16),
            v((2, 4, 224, 128), F32),
            v((2, 4, 224, 128), BF16),
            v((2, 4, 224, 128), BF16),
            v((2, 224, 128), BF16),
            v((2, 224, 128), BF16),
            v((448, 128), BF16),
            v((2, 224, 128), BF16),
            v((4, 3, 448, 128), BF16),
            v((4, 3, 448, 128), BF16),
            v((16, 32, 512), BF16),
            v((16, 32, 512), BF16),
            v((256, 1024), BF16),
            v((2, 4, 9, 16, 256), F32),
            v((2, 64, 256), F32),
            v((64, 256), F32),
            v((2, 64, 128), F32),
            v((64, 128), F32),
            v((64, 128), F32),
            v((27, 8, 512), F32),
            v((27, 32, 256), F32),
            pltpu.SemaphoreType.DMA((7,)),
            pltpu.SemaphoreType.DMA((NMSG,)),
            pltpu.SemaphoreType.DMA((NMSG,)),
        ],
        compiler_params=pltpu.CompilerParams(
            collective_id=0, has_side_effects=True, vmem_limit_bytes=60 * 1024 * 1024
        ),
        cost_estimate=pl.CostEstimate(flops=6_000_000_000, bytes_accessed=14_000_000, transcendentals=0),
        name="two_layers",
    )(
        volume,
        kernel_one.reshape(27 * 128, 512),
        kernel_two.reshape(27 * 512, 256),
        upstream.reshape(64, 128),
    )
    feat, g1, g2 = pl.pallas_call(
        place,
        out_shape=shapes,
        grid=(3,),
        in_specs=place_specs,
        out_specs=place_specs,
        name="place",
    )(*results)
    return feat.reshape(1, 8, 8, 128), g1, g2


def solution(mesh):
    return jax.shard_map(
        local,
        mesh=mesh,
        in_specs=(
            P("space", None, None, "chan"),
            P(None, "chan", "filt"),
            P(None, "filt", "chan"),
            P("space", None, None, ("chan", "filt")),
        ),
        out_specs=(
            P("space", None, None, ("chan", "filt")),
            P(None, ("chan", "space"), "filt"),
            P(None, ("filt", "space"), "chan"),
        ),
        check_vma=False,
    )
```

time: 88.1 us -> 70.5 us (0.80)
  Pallas kernels: 81.8 us -> 69.7 us
  local copies, waits for them, and re-layouts: 5.35 us -> 0 us
    pallas_call x1 -> x2, Pallas kernels: 81.8 us -> 69.7 us  [the longest x1 66.4 us: local(): pl.pallas_call(body, out_shape=shapes, in_specs=[any_spec] * 4, out_specs...]
    unnamed x3 -> x0, local copies, waits for them, and re-layouts: 5.35 us -> none
where the time goes in v2:
time: 70.5 us; the launch traced here: 70.3 us
  Pallas kernels  69.7 us (99%)
    pallas_call x1, Pallas kernels, local(): pl.pallas_call(body, out_shape=shapes, in_specs=[any_spec] * 4, out_specs...  66.4 us
    pallas_call x1, Pallas kernels, local(): pl.pallas_call(place, out_shape=shapes, grid=(3,), in_specs=place_specs,...  3.29 us

profile of v2, /device:TPU:0, one launch (start us, length us, event | category | flops | bytes accessed | tf_op | source)
XLA Modules:
  0.0 70.3 jit_solution(7044484881303066158)
XLA Ops:
  0.6 66.4 %two_layers.1 = (f32[64,128]{1,0:T(8,128)}, f32[27,8,512]{2,1,0:T(8,128)}, f32[27,32,256]{2,1,0:T(8,128)}) custom-call(bf16[4,32,32,128]{3,2,1,0:T(8,128)(2,1)} %vol.1, bf16[3456,512]{1,0:T(8,128)(2,1)} %bitcast.5, bf16[13824,256]{1,0:T(8,128)(2,1)} %bitcast.4, bf16[64,128]{1,0:T(8,128)(2,1)} %bitcast.7), custom_call_target="tpu_custom_call" | custom-call | flops 6000000000 | bytes 14000000 | tf_op jit(solution)/shard_map/two_layers/pallas_call | solution.py:456
  67.0 3.3 %place.1 = (f32[64,128]{1,0:T(8,128)}, f32[27,8,512]{2,1,0:T(8,128)}, f32[27,32,256]{2,1,0:T(8,128)}) custom-call(f32[64,128]{1,0:T(8,128)} %get-tuple-element.9.feat, f32[27,8,512]{2,1,0:T(8,128)} %get-tuple-element.10.g1, f32[27,32,256]{2,1,0:T(8,128)} %get-tuple-element.11.g2), custom_call_target="tpu_custom_call" | custom-call | tf_op jit(solution)/shard_map/place/pallas_call | solution.py:522

commit v3 on v2

--- a/solution.py
+++ b/solution.py
@@ -8,7 +8,7 @@
 SLOPE = 0.3
 F32, BF16 = jnp.float32, jnp.bfloat16
 MESH = pl.DeviceIdType.MESH
-NMSG = 80
+NMSG = 96
 
 
 def tap_parts(tap):
@@ -28,9 +28,9 @@
     vol, k1, k2, up, feat_o, g1_o, g2_o,
     vol_v, halo_v, k1_v, k2_v, pf, patch, patch_t,
     up_all, up_next, up_f, up_s, seed_s,
-    part, mr1, mr2, bpart, bs1, bs2, br1, br2,
+    part, mr1, mrf, mr2, bpart, bs1, bs2, br1, br2,
     hid, dlt,
-    acc, ksend, krecv, accx, xs4, xr4, xs1, xr1, ys1, yr1, ys2, yr2,
+    acc, ksend, krecv, accx, xs4, xr4, xs1, xr1, half_sum, ys1, yr1, ys2, yr2,
     gh, hh, hp, fs, fp, fr, fx, fxr, feat_v, g1_v, g2_v,
     lsem, ssem, rsem,
 ):
@@ -69,7 +69,7 @@
         pltpu.make_async_copy(k1, k1_v, lsem.at[2]),
         pltpu.make_async_copy(k2, k2_v, lsem.at[3]),
     ]
-    for copy in loads:
+    for copy in loads[0:3]:
         copy.start()
 
     barrier = pltpu.get_barrier_semaphore()
@@ -78,18 +78,19 @@
         pl.semaphore_signal(barrier, inc=1, device_id=device, device_id_type=MESH)
     pl.semaphore_wait(barrier, len(greeted))
 
-    send("halo", vol.at[3], halo_v, nxt)
     loads[1].wait()
     send("u0", up_all.at[h, s], up_all.at[h, s], hpt)
     send("u1", up_all.at[h, s], up_next.at[h], prv)
     send("u2", up_all.at[h, s], up_next.at[h], prv_h)
+    loads[0].wait()
+    send("halo", vol_v.at[3], halo_v, nxt)
+    loads[3].start()
 
     zero_row = jnp.zeros((40, 128), F32)
     zero_col = jnp.zeros((33, 8, 128), F32)
     for p in range(5):
         pf[p, 0] = zero_row
         pf[p, :, 0:8, :] = zero_col
-    loads[0].wait()
 
     def widen(r, carry):
         for p in range(4):
@@ -126,9 +127,10 @@
         part[second, rows, :] = both[:, 128:256]
 
     conv_one(2, 1, high)
-    send("m1m", part.at[2, high], mr1.at[1], zdn)
+    send("m1m", part.at[2, high], mr1, zdn)
     send("m2pb", part.at[1, high], mr2.at[0, high], zup)
     conv_one(3, 0, high)
+    build(0, (1, 2))
 
     up_f[...] = jnp.zeros_like(up_f)
 
@@ -142,10 +144,6 @@
     got("u0")
     got("u1")
     got("u2")
-    own_pair = up_all.at[:, s]
-    for d in range(1, 16):
-        send(f"a{d}", own_pair, own_pair, {"space": around[d]})
-
     def store_seed(later):
         def store(d, value):
             seed_s[later, d] = value
@@ -179,7 +177,6 @@
     bs2[1, 0:256] = bpart[zm, 0:256].astype(BF16)
     send("b2ma", bs2.at[1, low], br2.at[1, low], zdn)
 
-    build(0, (1, 2))
     got("halo")
 
     def widen_halo(r, carry):
@@ -189,21 +186,24 @@
     lax.fori_loop(0, 32, widen_halo, 0)
     build(0, (0,))
     conv_one(2, 3, low)
-    send("m1p", part.at[2, low], mr1.at[0], zup)
+    send("m1p", part.at[2, low], mrf, zup)
     send("m2ma", part.at[3, low], mr2.at[1, low], zdn)
+    own_pair = up_all.at[:, s]
+    for d in range(1, 16):
+        send(f"a{d}", own_pair, own_pair, {"space": around[d]})
     got("m1m")
-    part[3, 256:512] += mr1[1]
+    part[3, 256:512] += mr1[...]
     send("m2mb", part.at[3, high], mr2.at[1, high], zdn)
     conv_one(1, 0, low)
-    got("m1p")
-    part[1, 0:256] += mr1[0]
-    send("m2pa", part.at[1, low], mr2.at[0, low], zup)
     got("b1p")
     bs2[0, 0:256] = (bpart[zp, 0:256] + br1[0].astype(F32)).astype(BF16)
     send("b2pa", bs2.at[0, low], br2.at[0, low], zup)
     got("b1m")
     bs2[1, 256:512] = (bpart[zm, 256:512] + br1[1].astype(F32)).astype(BF16)
     send("b2mb", bs2.at[1, high], br2.at[1, high], zdn)
+    got("m1p")
+    part[1, 0:256] += mrf[...]
+    send("m2pa", part.at[1, low], mr2.at[0, low], zup)
 
     def put_turned(flat_rows, rows_at):
         for owner in range(16):
@@ -237,18 +237,25 @@
 
     lax.fori_loop(0, 16, shifted, 0)
 
-    for name in ("m2pb", "m2ma", "m2pa", "m2mb"):
+    for name in ("m2pb", "m2ma", "m2mb", "m2pa"):
         got(name)
     mixed = part[0] + mr2[0] + mr2[1]
     part[0] = mixed
     hid[:, lanes(z)] = jnp.where(mixed > 0, mixed, SLOPE * mixed).astype(BF16)
+    ways = (("p", zup, zp), ("m", zdn, zm), ("f", zfar, z2))
+
+    def quarter(v):
+        return hid.at[pl.ds(pl.multiple_of(v * 128, 128), 128), lanes(z)]
+
+    for way, device, v in ways:
+        send("e" + way, quarter(v), quarter(v), device)
     for name in ("b2pb", "b2ma", "b2pa", "b2mb"):
         got(name)
     back = bpart[z] + br2[0].astype(F32) + br2[1].astype(F32)
     dlt[:, lanes(z)] = (back * jnp.where(part[0] > 0, 1.0, SLOPE)).astype(BF16)
-    for tag, ref in (("d", dlt), ("h", hid)):
-        for way, device in (("p", zup), ("m", zdn), ("f", zfar)):
-            send(tag + way, ref.at[:, lanes(z)], ref.at[:, lanes(z)], device)
+    own_delta = dlt.at[:, lanes(z)]
+    send("dp", own_delta, own_delta, zup)
+    send("dm", own_delta, own_delta, zdn)
 
     def grad_one(slots):
         deltas = jnp.concatenate([dlt[:, lanes(lax.rem(z + slot, 4))] for slot in slots], 1)
@@ -310,9 +317,9 @@
     mine = pl.ds(pl.multiple_of(xl * 224, 32), 224)
     other = pl.ds(pl.multiple_of((1 - xl) * 224, 32), 224)
 
-    def put_grad_one(slot, value):
+    def put_grad_one(slot, value, first=0, last=27):
         q = lax.rem(z + slot, 4)
-        g1_v[:, :, lanes(q)] = value[0:216].reshape(27, 8, 128)
+        g1_v[first:last, :, lanes(q)] = value[0 : (last - first) * 8].reshape(last - first, 8, 128)
 
     def x_first(slot, lane):
         for n in range(4):
@@ -332,40 +339,87 @@
         got(f"x{slot}")
         put_grad_one(slot, acc[slot, y, mine] + xr1[lane].astype(F32))
 
+    def halved(v):
+        return jnp.concatenate([acc[2, v, 0:112], acc[2, v, 224:336]], 0)
+
+    def half_y():
+        for i, (v, device) in enumerate(((y2, yfar), (yp, yup), (ym, ydn))):
+            ys2[2, i, 0:224] = halved(v).astype(BF16)
+            send(f"y2{i}", ys2.at[2, i, 0:224], yr2.at[2, i, 0:224], device)
+
+    def half_y_sum():
+        for i in (1, 2, 0):
+            got(f"y2{i}")
+        total = halved(y)
+        for i in range(3):
+            total = total + yr2[2, i, 0:224].astype(F32)
+        for i in range(2):
+            half_sum[i] = total[i * 112 : (i + 1) * 112]
+        xs1[2, 0:112] = half_sum[1 - xl].astype(BF16)
+        send("x2", xs1.at[2, 0:112], xr1.at[2, 0:112], xpt)
+
+    def half_x():
+        rows = pl.ds(pl.multiple_of((1 - xl) * 224 + 112, 16), 112)
+        for n in range(4):
+            xs4[1, n, 0:112] = acc[2, n, rows].astype(BF16)
+        send("x4", xs4.at[1, :, 0:112], xr4.at[1, :, 0:112], xpt)
+
+    def half_x_sum():
+        got("x4")
+        rows = pl.ds(pl.multiple_of(xl * 224 + 112, 16), 112)
+        for n in range(4):
+            accx[1, n, 0:112] = acc[2, n, rows] + xr4[1, n, 0:112].astype(F32)
+        for i, (v, device) in enumerate(((y2, yfar), (yp, yup), (ym, ydn))):
+            ys2[1, i, 224:336] = accx[1, v, 0:112].astype(BF16)
+            send(f"y4{i}", ys2.at[1, i, 224:336], yr2.at[1, i, 224:336], device)
+
+    def half_x_done():
+        for i in (1, 2, 0):
+            got(f"y4{i}")
+        total = accx[1, y, 0:112]
+        for i in range(3):
+            total = total + yr2[1, i, 224:336].astype(F32)
+        put_grad_one(2, total, 14, 27)
+
     grad_one((0,))
+    send("df", own_delta, own_delta, zfar)
     add_sibling(0)
     ring_first(0, acc.at[0], 448)
+    for way, _, _ in ways:
+        got("e" + way)
+    cells = pl.ds(pl.multiple_of(z * 128, 128), 128)
+    flat = hid[cells, :].astype(F32).T.astype(BF16)
+    for owner in range(16):
+        gh[owner] = flat[owner * 32 : (owner + 1) * 32]
+    for d in range(1, 16):
+        send(f"g{d}", gh.at[around[d]], hh.at[z, s], {"space": around[d]})
+    hh[z, s] = gh[s]
     got("dp")
     got("dm")
+    for n in range(1, 4):
+        for way, device, v in ways:
+            block = quarter(lax.rem(v + n, 4))
+            send(f"h{way}{n}", block, block, device)
     grad_one((1, 3))
     ring_second(0, acc.at[0], 448)
     add_sibling(1)
     x_first(1, 0)
     add_sibling(3)
-    x_first(3, 1)
+    straight(3, acc.at[3], 448)
     got("df")
     grad_one((2,))
+    for d in range(1, 16):
+        got(f"g{d}")
+    for way, device, _ in ways:
+        send("v" + way, hh.at[z], hh.at[z], device)
     add_sibling(2)
-    straight(2, acc.at[2], 448)
+    half_x()
+    half_y()
     ring_third(0, acc.at[0], 448)
     x_last(0, 0)
-    x_second(1, 0)
-    straight(1, accx.at[0], 224)
-    x_second(3, 1)
-    straight(3, accx.at[1], 224)
-    for way in "pmf":
-        got("h" + way)
-
-    def turn_hidden(q, carry):
-        flat = hid[:, lanes(q)].astype(F32).T.astype(BF16)
-        for j in range(4):
-            gh[q * 4 + j] = flat[j * 32 : (j + 1) * 32]
-        return carry
-
-    lax.fori_loop(0, 4, turn_hidden, 0)
-    for d in range(1, 16):
-        send(f"g{d}", gh.at[around[d]], hh.at[s], {"space": around[d]})
-    hh[s] = gh[s]
+    for n in range(1, 4):
+        for way, _, _ in ways:
+            got(f"h{way}{n}")
 
     fs[...] = jnp.zeros_like(fs)
     for later in range(2):
@@ -392,24 +446,24 @@
         fp[later] = total.reshape(64, 256)
     send("f1", fp.at[1], fr, nxt)
 
-    straight_sum(2, acc.at[2], 448)
-    x_last(2, 1)
+    straight_sum(3, acc.at[3], 448)
+    x_last(3, 1)
+    x_second(1, 0)
+    straight(1, accx.at[0], 224)
+    half_y_sum()
+    half_x_sum()
     got("f1")
     whole = fp[0] + jnp.where(s > 0, fr[...], 0.0)
     for half in range(2):
         fx[half] = whole[:, half * 128 : (half + 1) * 128]
     send("f2", fx.at[1 - h], fxr, hpt)
-    straight_sum(1, accx.at[0], 224)
-    put_grad_one(1, accx[0, y])
-    straight_sum(3, accx.at[1], 224)
-    put_grad_one(3, accx[1, y])
-    x_done(0, 0)
-
-    for d in range(1, 16):
-        got(f"g{d}")
+
+    for way in "pmf":
+        got("v" + way)
     for phase in range(8):
+        zz, e = phase // 2, phase % 2
         for m in range(8):
-            two_slabs = [hh[2 * m + e, :, phase * 64 : (phase + 1) * 64] for e in range(2)]
+            two_slabs = [hh[zz, 2 * m + i, :, e * 64 : (e + 1) * 64] for i in range(2)]
             hp[phase * 32 : (phase + 1) * 32, m * 128 : (m + 1) * 128] = jnp.concatenate(two_slabs, 1)
     for do in range(2):
         for d in range(4):
@@ -421,7 +475,14 @@
                     g2_v[tap] = grads[phase * 32 : (phase + 1) * 32]
     stores = [pltpu.make_async_copy(g2_v, g2_o, lsem.at[4])]
     stores[0].start()
-    x_done(2, 1)
+
+    x_done(0, 0)
+    x_done(3, 1)
+    straight_sum(1, accx.at[0], 224)
+    put_grad_one(1, accx[0, y])
+    got("x2")
+    put_grad_one(2, half_sum[xl] + xr1[2, 0:112].astype(F32), 0, 14)
+    half_x_done()
     stores.append(pltpu.make_async_copy(g1_v, g1_o, lsem.at[5]))
     stores[1].start()
     got("f2")
@@ -472,7 +533,8 @@
             v((4, 1088, 256), BF16),
             v((2, 4, 64, 256), BF16),
             v((4, 512, 128), F32),
-            v((2, 256, 128), F32),
+            v((256, 128), F32),
+            v((256, 128), F32),
             v((2, 512, 128), F32),
             v((4, 512, 128), F32),
             v((512, 128), BF16),
@@ -487,14 +549,15 @@
             v((2, 4, 224, 128), F32),
             v((2, 4, 224, 128), BF16),
             v((2, 4, 224, 128), BF16),
-            v((2, 224, 128), BF16),
-            v((2, 224, 128), BF16),
+            v((3, 224, 128), BF16),
+            v((3, 224, 128), BF16),
+            v((2, 112, 128), F32),
             v((448, 128), BF16),
             v((2, 224, 128), BF16),
             v((4, 3, 448, 128), BF16),
             v((4, 3, 448, 128), BF16),
-            v((16, 32, 512), BF16),
-            v((16, 32, 512), BF16),
+            v((16, 32, 128), BF16),
+            v((4, 16, 32, 128), BF16),
             v((256, 1024), BF16),
             v((2, 4, 9, 16, 256), F32),
             v((2, 64, 256), F32),

time: 70.5 us -> 59.3 us (0.84)
  Pallas kernels: 69.7 us -> 58.4 us
    pallas_call x1, Pallas kernels: 66.4 us -> 55.1 us  [local(): pl.pallas_call(body, out_shape=shapes, in_specs=[any_spec] * 4, out_specs...]
where the time goes in v3:
time: 59.3 us; the launch traced here: 59.1 us
  Pallas kernels  58.4 us (98%)
  between operations  0.64 us (1%)
    pallas_call x1, Pallas kernels, local(): pl.pallas_call(body, out_shape=shapes, in_specs=[any_spec] * 4, out_specs...  55.1 us
    pallas_call x1, Pallas kernels, local(): pl.pallas_call(place, out_shape=shapes, grid=(3,), in_specs=place_specs,...  3.29 us

profile of v3, /device:TPU:0, one launch (start us, length us, event | category | flops | bytes accessed | tf_op | source)
XLA Modules:
  0.0 59.1 jit_solution(15542062436831394072)
XLA Ops:
  0.6 55.1 %two_layers.1 = (f32[64,128]{1,0:T(8,128)}, f32[27,8,512]{2,1,0:T(8,128)}, f32[27,32,256]{2,1,0:T(8,128)}) custom-call(bf16[4,32,32,128]{3,2,1,0:T(8,128)(2,1)} %vol.1, bf16[3456,512]{1,0:T(8,128)(2,1)} %bitcast.5, bf16[13824,256]{1,0:T(8,128)(2,1)} %bitcast.4, bf16[64,128]{1,0:T(8,128)(2,1)} %bitcast.7), custom_call_target="tpu_custom_call" | custom-call | flops 6000000000 | bytes 14000000 | tf_op jit(solution)/shard_map/two_layers/pallas_call | solution.py:517
  55.8 3.3 %place.1 = (f32[64,128]{1,0:T(8,128)}, f32[27,8,512]{2,1,0:T(8,128)}, f32[27,32,256]{2,1,0:T(8,128)}) custom-call(f32[64,128]{1,0:T(8,128)} %get-tuple-element.9.feat, f32[27,8,512]{2,1,0:T(8,128)} %get-tuple-element.10.g1, f32[27,32,256]{2,1,0:T(8,128)} %get-tuple-element.11.g2), custom_call_target="tpu_custom_call" | custom-call | tf_op jit(solution)/shard_map/place/pallas_call | solution.py:585

commit v4 on v3

--- a/solution.py
+++ b/solution.py
@@ -222,20 +222,6 @@
     lax.fori_loop(0, 13, turn, 0)
     flat = patch[:, 26 * 128 : 27 * 128].astype(F32).T
     put_turned(lambda owner: jnp.concatenate([flat[owner * 8 : owner * 8 + 8], jnp.zeros((8, 512), F32)], 0), 208)
-
-    for d in range(4):
-        up_s[d, 1024:1088, :] = jnp.zeros((64, 256), BF16)
-    for d in range(1, 16):
-        got(f"a{d}")
-
-    def shifted(slab, carry):
-        def store(d, value):
-            up_s[d, pl.ds(pl.multiple_of(slab * 64, 64), 64), :] = value
-
-        moved([up_all[half, slab] for half in range(2)], store)
-        return carry
-
-    lax.fori_loop(0, 16, shifted, 0)
 
     for name in ("m2pb", "m2ma", "m2mb", "m2pa"):
         got(name)
@@ -417,6 +403,20 @@
     half_y()
     ring_third(0, acc.at[0], 448)
     x_last(0, 0)
+    for d in range(4):
+        up_s[d, 1024:1088, :] = jnp.zeros((64, 256), BF16)
+    for d in range(1, 16):
+        got(f"a{d}")
+
+    def shifted(slab, carry):
+        def store(d, value):
+            up_s[d, pl.ds(pl.multiple_of(slab * 64, 64), 64), :] = value
+
+        moved([up_all[half, slab] for half in range(2)], store)
+        return carry
+
+    lax.fori_loop(0, 16, shifted, 0)
+
     for n in range(1, 4):
         for way, _, _ in ways:
             got(f"h{way}{n}")
@@ -495,10 +495,13 @@
         copy.wait()
 
 
-def place(feat, g1, g2, feat_o, g1_o, g2_o):
-    feat_o[...] = feat[...]
-    g1_o[...] = g1[...]
-    g2_o[...] = g2[...]
+def place(*refs):
+    sources, targets, sems = refs[0:3], refs[3:6], refs[6]
+    copies = [pltpu.make_async_copy(a, b, sems.at[i]) for i, (a, b) in enumerate(zip(sources, targets))]
+    for copy in copies:
+        copy.start()
+    for copy in copies:
+        copy.wait()
 
 
 def local(volume, kernel_one, kernel_two, upstream):
@@ -508,11 +511,6 @@
         jax.ShapeDtypeStruct((64, 128), F32),
         jax.ShapeDtypeStruct((27, 8, 512), F32),
         jax.ShapeDtypeStruct((27, 32, 256), F32),
-    )
-    place_specs = (
-        pl.BlockSpec((64, 128), lambda i: (0, 0)),
-        pl.BlockSpec((9, 8, 512), lambda i: (i, 0, 0)),
-        pl.BlockSpec((9, 32, 256), lambda i: (i, 0, 0)),
     )
     results = pl.pallas_call(
         body,
@@ -585,9 +583,9 @@
     feat, g1, g2 = pl.pallas_call(
         place,
         out_shape=shapes,
-        grid=(3,),
-        in_specs=place_specs,
-        out_specs=place_specs,
+        in_specs=[pl.BlockSpec(memory_space=pltpu.VMEM)] * 3,
+        out_specs=(any_spec,) * 3,
+        scratch_shapes=[pltpu.SemaphoreType.DMA((3,))],
         name="place",
     )(*results)
     return feat.reshape(1, 8, 8, 128), g1, g2

time: 59.3 us -> 58.4 us (0.985)
  Pallas kernels: 58.4 us -> 57.6 us
    pallas_call x1, Pallas kernels: 3.29 us -> 2.42 us  [local(): pl.pallas_call(place, out_shape=shapes, in_specs=[pl.BlockSpec(memory_spa...]
where the time goes in v4:
time: 58.4 us; the launch traced here: 58.2 us
  Pallas kernels  57.6 us (99%)
  between operations  0.64 us (1%)
    pallas_call x1, Pallas kernels, local(): pl.pallas_call(body, out_shape=shapes, in_specs=[any_spec] * 4, out_specs...  55.1 us
    pallas_call x1, Pallas kernels, local(): pl.pallas_call(place, out_shape=shapes, in_specs=[pl.BlockSpec(memory_spa...  2.42 us

profile of v4, /device:TPU:0, one launch (start us, length us, event | category | flops | bytes accessed | tf_op | source)
XLA Modules:
  0.0 58.2 jit_solution(11249327591112506722)
XLA Ops:
  0.6 55.1 %two_layers.1 = (f32[64,128]{1,0:T(8,128)}, f32[27,8,512]{2,1,0:T(8,128)}, f32[27,32,256]{2,1,0:T(8,128)}) custom-call(bf16[4,32,32,128]{3,2,1,0:T(8,128)(2,1)} %vol.1, bf16[3456,512]{1,0:T(8,128)(2,1)} %bitcast.5, bf16[13824,256]{1,0:T(8,128)(2,1)} %bitcast.4, bf16[64,128]{1,0:T(8,128)(2,1)} %bitcast.7), custom_call_target="tpu_custom_call" | custom-call | flops 6000000000 | bytes 14000000 | tf_op jit(solution)/shard_map/two_layers/pallas_call | solution.py:515
  55.8 2.4 %place.1 = (f32[64,128]{1,0:T(8,128)}, f32[27,8,512]{2,1,0:T(8,128)}, f32[27,32,256]{2,1,0:T(8,128)}) custom-call(f32[64,128]{1,0:T(8,128)} %get-tuple-element.9.refs_0_, f32[27,8,512]{2,1,0:T(8,128)} %get-tuple-element.10.refs_1_, f32[27,32,256]{2,1,0:T(8,128)} %get-tuple-element.11.refs_2_), custom_call_target="tpu_custom_call" | custom-call | tf_op jit(solution)/shard_map/place/pallas_call | solution.py:583
